TPU v7x, 32 devices: a whole 2x2x4 slice. The times are simulated.
32 devices in a mesh: blk: 16 (over z, y, x), seg: 2 (over core).
Axes of the slice: x: 2, y: 2, z: 4, core: 2. Of those that a mesh axis runs over, the one named last changes fastest.
Arguments:
- spectra: bfloat16 [28, 2048, 2, 512], P('seg', 'blk'), as said below
- valid_flags: int32 [28, 2048], P('seg', 'blk'), may hold values 0 or 1
Outputs:
- correlations: bfloat16 [2, 2048, 128, 1024], P(None, ('blk', 'seg'))
Inputs may be any that keep to these rules, and one draw needn't show every extreme that they name: `spectra`: rough spectral values; their scale varies from bin to bin, channel to channel and window to window.
All inputs are finite; a program needn't handle non-finite values. No bound on the sum of `valid_flags` on one device may be relied on, other than what follows from the above.
Results may differ from a plain program's by a relative error of at most 0.015.
Values may be sent and summed in bfloat16 or wider, within the bound.
A program may use at most 192 MiB of HBM per device.

v0:
```python
import math

import jax
import jax.numpy as jnp
from jax import lax
from jax.sharding import PartitionSpec as P

LAG_COUNT = 1024
WIN_SAMPLES = 15000
BAND_START = 30
SMOOTH_HALF = 32
ROUNDS = 2


def passed_along(value, axis, steps):
    count = lax.axis_size(axis)
    pairs = [(source, (source + steps) % count) for source in range(count)]
    return lax.ppermute(value, axis, pairs)


def lag_table(bin_count, lag_count):
    freq_ids = lax.broadcasted_iota(jnp.int32, (bin_count, lag_count), 0) + BAND_START
    delay_ids = lax.broadcasted_iota(jnp.int32, (bin_count, lag_count), 1) - lag_count // 2
    angles = jnp.mod(freq_ids * delay_ids, WIN_SAMPLES).astype(jnp.float32) * (
        2.0 * math.pi / WIN_SAMPLES
    )
    return jnp.stack([jnp.cos(angles), -jnp.sin(angles)], axis=1).astype(jnp.bfloat16)


def whiten(spectra, valid_flags):
    bin_count = spectra.shape[3]
    real_part = spectra[:, :, 0, :].astype(jnp.float32)
    imag_part = spectra[:, :, 1, :].astype(jnp.float32)
    amplitude = jnp.sqrt(real_part * real_part + imag_part * imag_part).astype(jnp.bfloat16)
    row_ids = lax.broadcasted_iota(jnp.int32, (bin_count, bin_count), 0)
    col_ids = lax.broadcasted_iota(jnp.int32, (bin_count, bin_count), 1)
    band_mask = jnp.abs(row_ids - col_ids) <= SMOOTH_HALF
    counts = jnp.sum(band_mask.astype(jnp.float32), axis=0)
    summed = jnp.dot(
        amplitude.reshape(-1, bin_count),
        band_mask.astype(jnp.bfloat16),
        preferred_element_type=jnp.float32,
    )
    smooth = summed.reshape(amplitude.shape) / counts
    scaling = valid_flags.astype(jnp.float32)[:, :, None] / (smooth + 1e-05)
    whitened = (spectra.astype(jnp.float32) * scaling[:, :, None, :]).astype(jnp.bfloat16)
    return jnp.transpose(whitened, (3, 2, 0, 1))


def cross_terms(owned, partner):
    rotated = jnp.stack([-partner[:, 1], partner[:, 0]], axis=1)
    joined = jnp.concatenate([partner, rotated], axis=3)
    return lax.dot_general(
        owned, joined, (((1, 2), (1, 2)), ((0,), (0,))), preferred_element_type=jnp.float32
    )


def invert(received, table, scaling):
    bin_count, rows_here, doubled = received.shape
    stack = received.astype(jnp.bfloat16).reshape(bin_count, rows_here, 2, doubled // 2)
    result = lax.dot_general(
        stack, table, (((0, 2), (0, 1)), ((), ())), preferred_element_type=jnp.float32
    )
    return (result * scaling).astype(jnp.bfloat16)


def shards(spectra, valid_flags):
    seg_count = lax.axis_size("seg")
    windows_here = spectra.shape[0]
    bin_count = spectra.shape[3]
    table = lag_table(bin_count, LAG_COUNT)
    scaling = 1.0 / math.sqrt(windows_here * seg_count * bin_count)
    owned = whiten(spectra, valid_flags)
    previous_white = owned
    results = []
    for rounds_done in range(ROUNDS):
        stride = rounds_done + 1
        previous_white = passed_along(owned, "blk", stride)
        partials = cross_terms(owned, previous_white)
        received = lax.psum_scatter(
            partials.astype(jnp.bfloat16), "seg", scatter_dimension=1, tiled=True
        ).astype(jnp.float32)
        results.append(invert(received, table, scaling))
    return jnp.stack(results)


def solution(mesh):
    in_specs = (P("seg", "blk", None, None), P("seg", "blk"))
    out_specs = P(None, ("blk", "seg"), None, None)
    return jax.shard_map(shards, mesh=mesh, in_specs=in_specs, out_specs=out_specs, check_vma=False)
```

profile of v0, /device:TPU:0, one launch (start us, length us, event | category | flops | bytes accessed | tf_op | source)
XLA Modules:
  0.0 397.7 jit_solution(13735001770429143747)
XLA Ops:
  6.5 0.0 reduce-scatter.5.cloned.1.call-start
  6.5 0.1 convert_reduce_fusion
  6.6 9.9 %copy.13 = bf16[14,128,2,512]{1,3,0,2:T(8,128)(2,1)} copy(bf16[14,128,2,512]{3,2,1,0:T(2,128)(2,1)} %param.2) | data formatting | bytes 7340032 | tf_op args[0]
  16.6 8.1 %fusion.38 = (bf16[14,128,1,512]{3,2,1,0:T(2,128)(2,1)S(1)}, bf16[14,128,1,512]{3,2,1,0:T(2,128)(2,1)S(1)}) fusion(bf16[14,128,2,512]{3,2,1,0:T(2,128)(2,1)} %param.2), kind=kLoop, calls=%fused_computation.52 | loop fusion | bytes 7340032 | tf_op jit(solution)/shard_map/slice | solution.py:32
  24.7 0.0 copy-done.3
  24.7 3.6 add_divide_fusion
  28.3 5.1 %copy.16 = f32[14,128,512]{1,2,0:T(8,128)} copy(f32[14,128,512]{2,1,0:T(8,128)} %add_divide_fusion) | data formatting | bytes 7340032 | tf_op jit(solution)/shard_map/div | solution.py:45
  33.4 4.1 %fusion.16 = bf16[512,2,14,128]{3,0,2,1:T(8,128)(2,1)S(1)} fusion(bf16[14,128,2,512]{1,3,0,2:T(8,128)(2,1)} %copy.13, f32[14,128,512]{1,2,0:T(8,128)} %copy.16), kind=kLoop, calls=%fused_computation.22 | loop fusion | flops 5505024 | bytes 11010048 | tf_op jit(solution)/shard_map/transpose | solution.py:47
  37.6 0.0 copy-start
  37.6 3.0 collective-permute-start.1
  40.6 82.4 %collective-permute-done.1 = bf16[512,2,14,128]{3,0,2,1:T(8,128)(2,1)S(1)} collective-permute-done((bf16[512,2,14,128]{3,0,2,1:T(8,128)(2,1)S(1)}, bf16[512,2,14,128]{3,0,2,1:T(8,128)(2,1)S(1)}, u32[]{:S(2)}, u32[]{:S(2)}) %collective-permute-start.1) | collective-permute-done | bytes 3670048 | tf_op jit(solution)/shard_map/ppermute | solution.py:18
  123.0 2.4 copy.24
  125.4 0.0 copy-done
  125.4 2.0 slice_negate_fusion
  127.4 0.6 copy-done.2
  128.0 18.0 %bitcast_convert_fusion = bf16[512,128,256]{2,1,0:T(8,128)(2,1)} fusion(bf16[512,1,14,128]{3,2,1,0:T(8,128)(2,1)} %get-tuple-element.8, bf16[512,1,14,128]{3,2,1,0:T(8,128)(2,1)S(1)} %get-tuple-element.7, bf16[512,2,14,128]{3,2,1,0:T(8,128)(2,1)} %copy-done.2, bf16[512,2,14,128]{3,0,2,1:T(8,128)(2,1)} %copy-done), kind=kOutput, calls=%fused_computation | convolution fusion | flops 978321408 | bytes 44564480 | tf_op jit(solution)/shard_map/dot_general | solution.py:53
  146.0 0.0 reduce-scatter.5.cloned.1.call-update
  146.0 0.0 reduce-scatter.3.cloned.1.call-start
  146.1 1.7 collective-permute-start
  147.8 82.8 %collective-permute-done = bf16[512,2,14,128]{3,0,2,1:T(8,128)(2,1)S(1)} collective-permute-done((bf16[512,2,14,128]{3,0,2,1:T(8,128)(2,1)}, bf16[512,2,14,128]{3,0,2,1:T(8,128)(2,1)S(1)}, u32[]{:S(2)}, u32[]{:S(2)}) %collective-permute-start) | collective-permute-done | bytes 3670048 | tf_op jit(solution)/shard_map/ppermute | solution.py:18
  230.6 2.4 copy.19
  233.1 2.0 slice_negate_fusion.1
  235.1 0.6 copy-done.1
  235.7 17.7 %bitcast_convert_fusion.1 = bf16[512,128,256]{2,1,0:T(8,128)(2,1)} fusion(bf16[512,1,14,128]{3,2,1,0:T(8,128)(2,1)} %get-tuple-element.6, bf16[512,1,14,128]{3,2,1,0:T(8,128)(2,1)S(1)} %get-tuple-element.5, bf16[512,2,14,128]{3,2,1,0:T(8,128)(2,1)} %copy-done.1, bf16[512,2,14,128]{3,0,2,1:T(8,128)(2,1)} %copy-done), kind=kOutput, calls=%fused_computation.1 | convolution fusion | flops 978321408 | bytes 44564480 | tf_op jit(solution)/shard_map/dot_general | solution.py:53
  253.4 0.0 reduce-scatter.3.cloned.1.call-update
  253.5 9.3 %cosine_convert_fusion = (bf16[512,1,1024]{2,0,1:T(8,128)(2,1)S(1)}, bf16[512,1,1024]{2,0,1:T(8,128)(2,1)S(1)}) fusion(s32[1024]{0:T(1024)S(1)} %iota_add_fusion, s32[512]{0:T(512)S(1)} %iota_add_fusion.1), kind=kLoop, calls=%fused_computation.32 | loop fusion | flops 6291456 | bytes 2103296 | tf_op jit(solution)/shard_map/convert
  262.8 0.0 reduce-scatter.5.cloned.1.call-done
  262.8 26.7 %copy.32 = bf16[512,64,256]{0,2,1:T(8,128)(2,1)} copy(bf16[512,64,256]{2,1,0:T(8,128)(2,1)} %reduce-scatter.5.cloned.1.call-done) | data formatting | bytes 33554432 | tf_op jit(solution)/shard_map/reshape | solution.py:60
  289.5 27.6 %fusion.3 = bf16[1,64,128,1024]{3,2,1,0:T(8,128)(2,1)} fusion(bf16[512,64,2,128]{0,3,2,1:T(8,128)(2,1)} %bitcast.45, bf16[512,1,1024]{2,0,1:T(8,128)(2,1)S(1)} %get-tuple-element.12, bf16[512,1,1024]{2,0,1:T(8,128)(2,1)S(1)} %get-tuple-element.11), kind=kOutput, calls=%fused_computation.8 | convolution fusion | flops 17197694976 | bytes 35651584 | tf_op jit(solution)/shard_map/dot_general | solution.py:61
  317.1 24.7 %copy.31 = bf16[512,64,256]{0,2,1:T(8,128)(2,1)} copy(bf16[512,64,256]{2,1,0:T(8,128)(2,1)} %reduce-scatter.3.cloned.1.call-done) | data formatting | bytes 33554432 | tf_op jit(solution)/shard_map/reshape | solution.py:60
  341.8 26.1 %fusion.2 = bf16[1,64,128,1024]{3,2,1,0:T(8,128)(2,1)} fusion(bf16[512,64,2,128]{0,3,2,1:T(8,128)(2,1)} %bitcast.44, bf16[512,1,1024]{2,0,1:T(8,128)(2,1)S(1)} %get-tuple-element.12, bf16[512,1,1024]{2,0,1:T(8,128)(2,1)S(1)} %get-tuple-element.11), kind=kOutput, calls=%fused_computation.7 | convolution fusion | flops 17197694976 | bytes 35651584 | tf_op jit(solution)/shard_map/dot_general | solution.py:61
  367.9 23.0 %pad_maximum_fusion = bf16[2,64,128,1024]{3,2,1,0:T(8,128)(2,1)} fusion(bf16[1,64,128,1024]{3,2,1,0:T(8,128)(2,1)} %fusion.3, bf16[1,64,128,1024]{3,2,1,0:T(8,128)(2,1)} %fusion.2), kind=kLoop, calls=%fused_computation.2 | loop fusion | flops 16777216 | bytes 67108864 | tf_op jit(solution)/shard_map/stack | solution.py:84
  (7 shorter events, 0.0 us)
Async XLA Ops:
  6.5 256.3 %reduce-scatter.5.cloned.1.call-start = ((), (), s32[]{:S(2)}) async-start(), calls=%async_computation.3 | async-start | bytes 50331648 | tf_op jit(solution)/shard_map/reduce_scatter | solution.py:80
  16.6 8.1 %copy-start.3 = (s32[14,128]{1,0:T(8,128)S(1)}, s32[14,128]{1,0:T(8,128)}, u32[]{:S(2)}) copy-start(s32[14,128]{1,0:T(8,128)} %param.3) | copy-start | bytes 21508
  37.6 87.8 %copy-start = (bf16[512,2,14,128]{3,0,2,1:T(8,128)(2,1)}, bf16[512,2,14,128]{3,0,2,1:T(8,128)(2,1)S(1)}, u32[]{:S(2)}) copy-start(bf16[512,2,14,128]{3,0,2,1:T(8,128)(2,1)S(1)} %fusion.16) | copy-start | bytes 11010052
  37.6 85.4 %collective-permute-start.1 = (bf16[512,2,14,128]{3,0,2,1:T(8,128)(2,1)S(1)}, bf16[512,2,14,128]{3,0,2,1:T(8,128)(2,1)S(1)}, u32[]{:S(2)}, u32[]{:S(2)}) collective-permute-start(bf16[512,2,14,128]{3,0,2,1:T(8,128)(2,1)S(1)} %fusion.16), channel_id=1, source_target_pairs={{0,4},{2,6},{4,8},{6,10},{8,12},{10,14},{12,16},{14,18},{16,20},{1... | collective-permute-start | bytes 11010056 | tf_op jit(solution)/shard_map/ppermute | solution.py:18
  125.4 2.6 copy-start.2
  146.0 171.1 %reduce-scatter.3.cloned.1.call-start = ((), (), s32[]{:S(2)}) async-start(), calls=%async_computation.2 | async-start | bytes 50331648 | tf_op jit(solution)/shard_map/reduce_scatter | solution.py:80
  146.1 84.6 %collective-permute-start = (bf16[512,2,14,128]{3,0,2,1:T(8,128)(2,1)}, bf16[512,2,14,128]{3,0,2,1:T(8,128)(2,1)S(1)}, u32[]{:S(2)}, u32[]{:S(2)}) collective-permute-start(bf16[512,2,14,128]{3,0,2,1:T(8,128)(2,1)} %copy-done), channel_id=1, source_target_pairs={{0,2},{2,4},{4,6},{6,8},{8,10},{10,12},{12,14},{14,16},{16,18},{18... | collective-permute-start | bytes 11010056 | tf_op jit(solution)/shard_map/ppermute | solution.py:18
  233.1 2.6 copy-start.1
Sparse Core Ops, SparseCore 0:
  146.2 43.6 reduce-scatter.4
  253.6 41.0 reduce-scatter.2
where the time goes:
time: 399 us; the launch traced here: 398 us
  waiting for transfers between devices  165 us (41%)
  matrix products  93 us (23%)
  local copies, waits for them, and re-layouts  80.6 us (20%)
  other arithmetic  40.5 us (10%)
  between operations  13.5 us (3%)
  starting transfers between devices  4.8 us (1%)
    ppermute x2, waiting for transfers between devices, passed_along(): return lax.ppermute(value, axis, pairs)  165 us
    dot_general x2, matrix products, invert(): lax.dot_general(stack, table, (((0, 2), (0, 1)), ((), ())), preferred_ele...  53.7 us
    reshape x2, local copies, waits for them, and re-layouts, invert(): received.astype(jnp.bfloat16).reshape(bin_count, rows_here, 2, doubled // 2)  51.4 us
    dot_general x2, matrix products, cross_terms(): lax.dot_general(owned, joined, (((1, 2), (1, 2)), ((0,), (0,))), preferre...  35.7 us
    another operation x1, other arithmetic, shards(): return jnp.stack(results)  23 us
    unnamed x9, local copies, waits for them, and re-layouts  11.2 us
    another operation x1, other arithmetic  9.29 us
    slice x1, local copies, waits for them, and re-layouts, whiten(): real_part = spectra[:, :, 0, :].astype(jnp.float32)  8.1 us
  transfers between devices with their start and end apart: 4, of which 2 were waited for; matrix products, arithmetic and copies ran while one was open for 22% of the time, Pallas kernels for 0%

commit v1 on v0

--- a/solution.py
+++ b/solution.py
@@ -1,8 +1,11 @@
+import functools
 import math
 
 import jax
 import jax.numpy as jnp
 from jax import lax
+from jax.experimental import pallas as pl
+from jax.experimental.pallas import tpu as pltpu
 from jax.sharding import PartitionSpec as P
 
 LAG_COUNT = 1024
@@ -64,7 +67,7 @@
     return (result * scaling).astype(jnp.bfloat16)
 
 
-def shards(spectra, valid_flags):
+def shards_plain(spectra, valid_flags):
     seg_count = lax.axis_size("seg")
     windows_here = spectra.shape[0]
     bin_count = spectra.shape[3]
@@ -84,6 +87,258 @@
     return jnp.stack(results)
 
 
+PIECES = 8
+ROW_GROUP = 4
+MESH = pl.DeviceIdType.MESH
+
+
+def exchange_kernel(blk_count, seg_count, own, gathered, own_all, transit, local_sem, near_send,
+                    near_recv, seg_send, seg_recv):
+    blk, seg = lax.axis_index("blk"), lax.axis_index("seg")
+    place = lax.rem(blk, 4)
+    low, high = lax.rem(place, 2), place // 2
+    across_x = blk + 1 - 2 * low
+    across_y = blk + 2 - 4 * high
+    up_z = lax.rem(blk + 4, blk_count)
+    down_z = lax.rem(blk + blk_count - 4, blk_count)
+    siblings = [lax.rem(seg + k, seg_count) for k in range(1, seg_count)]
+    bins = own.shape[0] // PIECES
+    barrier = pltpu.get_barrier_semaphore()
+
+    def greet(target_blk, target_seg):
+        pl.semaphore_signal(barrier, inc=1, device_id=(target_blk, target_seg), device_id_type=MESH)
+
+    greet(across_x, seg)
+    greet(across_y, seg)
+    for sibling in siblings:
+        greet(blk, sibling)
+
+    @pl.when(high == 1)
+    def _():
+        greet(up_z, seg)
+        greet(down_z, seg)
+
+    pl.semaphore_wait(barrier, 2 + len(siblings) + 2 * high)
+
+    def part(k):
+        return pl.ds(k * bins, bins)
+
+    def near(src, dst, send_row, recv_row, k, target):
+        return pltpu.make_async_remote_copy(
+            src_ref=src, dst_ref=dst, send_sem=near_send.at[send_row, k],
+            recv_sem=near_recv.at[recv_row, k], device_id=(target, seg), device_id_type=MESH)
+
+    def own_x(k):
+        return near(own.at[part(k)], gathered.at[0, seg, part(k)], 0, 0, k, across_x)
+
+    def own_y(k):
+        return near(own.at[part(k)], gathered.at[1, seg, part(k)], 1, 1, k, across_y)
+
+    def own_z(k):
+        return near(own.at[part(k)], transit.at[part(k)], 2, 2, k, up_z)
+
+    def forward_y(k):
+        return near(transit.at[part(k)], gathered.at[1, seg, part(k)], 3, 1, k, across_y)
+
+    def forward_x(k):
+        return near(gathered.at[1, seg, part(k)], gathered.at[0, seg, part(k)], 4, 0, k, across_x)
+
+    def share(src, dst, row, k, n):
+        return pltpu.make_async_remote_copy(
+            src_ref=src, dst_ref=dst, send_sem=seg_send.at[row, k, n],
+            recv_sem=seg_recv.at[row, k, n], device_id=(blk, siblings[n]), device_id_type=MESH)
+
+    def share_round(r, k, n):
+        piece = gathered.at[r, seg, part(k)]
+        return share(piece, piece, r, k, n)
+
+    def landed_round(r, k, n):
+        piece = gathered.at[r, lax.rem(seg + seg_count - n - 1, seg_count), part(k)]
+        return share(piece, piece, r, k, n)
+
+    def share_own(k, n):
+        return share(own.at[part(k)], own_all.at[seg, part(k)], 2, k, n)
+
+    def landed_own(k, n):
+        piece = own_all.at[lax.rem(seg + seg_count - n - 1, seg_count), part(k)]
+        return share(piece, piece, 2, k, n)
+
+    firsts = ((low == 0, own_x), (high == 0, own_y), (high == 1, own_z))
+
+    def start_own(k):
+        for condition, make in firsts:
+            @pl.when(condition)
+            def _(make=make):
+                make(k).start()
+
+    def wait_own(k):
+        for condition, make in firsts:
+            @pl.when(condition)
+            def _(make=make):
+                make(k).wait_send()
+
+    start_own(0)
+    start_own(1)
+    local = pltpu.make_async_copy(own, own_all.at[seg], local_sem)
+    local.start()
+    for k in range(PIECES):
+        for n in range(len(siblings)):
+            share_own(k, n).start()
+    for k in range(PIECES + 1):
+        if k < PIECES:
+            wait_own(k)
+            if k + 2 < PIECES:
+                start_own(k + 2)
+
+            @pl.when(high == 1)
+            def _():
+                own_z(k).wait_recv()
+                forward_y(k).start()
+
+            own_y(k).wait_recv()
+
+            @pl.when(low == 1)
+            def _():
+                forward_x(k).start()
+
+            for n in range(len(siblings)):
+                share_round(1, k, n).start()
+        if k >= 1:
+            own_x(k - 1).wait_recv()
+            for n in range(len(siblings)):
+                share_round(0, k - 1, n).start()
+    for k in range(PIECES):
+        @pl.when(high == 1)
+        def _():
+            forward_y(k).wait_send()
+
+        @pl.when(low == 1)
+        def _():
+            forward_x(k).wait_send()
+
+        for n in range(len(siblings)):
+            for r in range(ROUNDS):
+                share_round(r, k, n).wait_send()
+                landed_round(r, k, n).wait_recv()
+            share_own(k, n).wait_send()
+            landed_own(k, n).wait_recv()
+    local.wait()
+
+
+def exchange(own, blk_count, seg_count):
+    others = max(seg_count - 1, 1)
+    anywhere = pl.BlockSpec(memory_space=pl.ANY)
+    gathered, own_all, _ = pl.pallas_call(
+        functools.partial(exchange_kernel, blk_count, seg_count),
+        out_shape=(
+            jax.ShapeDtypeStruct((ROUNDS, seg_count, *own.shape), own.dtype),
+            jax.ShapeDtypeStruct((seg_count, *own.shape), own.dtype),
+            jax.ShapeDtypeStruct(own.shape, own.dtype),
+        ),
+        in_specs=[anywhere],
+        out_specs=(anywhere,) * 3,
+        scratch_shapes=[
+            pltpu.SemaphoreType.DMA,
+            pltpu.SemaphoreType.DMA((5, PIECES)),
+            pltpu.SemaphoreType.DMA((3, PIECES)),
+            pltpu.SemaphoreType.DMA((3, PIECES, others)),
+            pltpu.SemaphoreType.DMA((3, PIECES, others)),
+        ],
+        compiler_params=pltpu.CompilerParams(
+            collective_id=0, has_side_effects=True, vmem_limit_bytes=60 * 2**20),
+    )(own)
+    return gathered, own_all
+
+
+def correlate_kernel(chunk_count, scaling, own_ref, partner_ref, table_ref, out_ref, cross, left):
+    step = pl.program_id(1)
+    bins_here, rows, _ = own_ref.shape
+    width = partner_ref.shape[-1]
+    bin_count = cross.shape[1] // rows
+    group = out_ref.shape[1]
+
+    @pl.when(step < chunk_count)
+    def _():
+        @pl.loop(0, bins_here, unroll=8)
+        def _(f):
+            segments = partner_ref.shape[1]
+            real = jnp.concatenate([partner_ref[0, s, f, 0] for s in range(segments)], axis=0)
+            imag = jnp.concatenate([partner_ref[0, s, f, 1] for s in range(segments)], axis=0)
+            joined = jnp.concatenate(
+                [jnp.concatenate([real, -imag], axis=1), jnp.concatenate([imag, real], axis=1)], axis=0)
+            result = jnp.dot(own_ref[f], joined, preferred_element_type=jnp.float32)
+            start = pl.multiple_of((step * bins_here + f) * rows, 8)
+            cross[0, pl.ds(start, rows), :] = result[:, :width]
+            cross[1, pl.ds(start, rows), :] = result[:, width:]
+
+    @pl.when(step >= chunk_count)
+    def _():
+        first = (step - chunk_count) * group
+        for n in range(group):
+            for k in range(2):
+                picked = cross[k, pl.ds(first + n, bin_count, stride=rows), :]
+                left[n * width:(n + 1) * width, k * bin_count:(k + 1) * bin_count] = (
+                    picked.astype(jnp.bfloat16).T)
+        lags = table_ref.shape[1]
+        span = 256
+
+        @pl.loop(0, lags // span, unroll=True)
+        def _(c):
+            columns = pl.ds(pl.multiple_of(c * span, span), span)
+            result = jnp.dot(left[...], table_ref[:, columns], preferred_element_type=jnp.float32)
+            out_ref[0, :, :, columns] = (result * scaling).astype(jnp.bfloat16).reshape(
+                group, width, span)
+
+
+def correlate(own, gathered, table, scaling):
+    bin_count, rows, depth = own.shape
+    rounds, seg_count, _, _, windows, width = gathered.shape
+    lags = table.shape[1]
+    bins_here = bin_count // 16
+    chunk_count = bin_count // bins_here
+    group = ROW_GROUP
+    steps = chunk_count + rows // group
+    return pl.pallas_call(
+        functools.partial(correlate_kernel, chunk_count, scaling),
+        grid=(rounds, steps),
+        out_shape=jax.ShapeDtypeStruct((rounds, rows, width, lags), jnp.bfloat16),
+        in_specs=[
+            pl.BlockSpec((bins_here, rows, depth), lambda r, t: (jnp.minimum(t, chunk_count - 1), 0, 0)),
+            pl.BlockSpec((1, seg_count, bins_here, 2, windows, width),
+                         lambda r, t: (r, 0, jnp.minimum(t, chunk_count - 1), 0, 0, 0)),
+            pl.BlockSpec((2 * bin_count, lags), lambda r, t: (0, 0)),
+        ],
+        out_specs=pl.BlockSpec((1, group, width, lags),
+                               lambda r, t: (r, jnp.maximum(t - chunk_count, 0), 0, 0)),
+        scratch_shapes=[
+            pltpu.VMEM((2, bin_count * rows, width), jnp.float32),
+            pltpu.VMEM((group * width, 2 * bin_count), jnp.bfloat16),
+        ],
+        compiler_params=pltpu.CompilerParams(vmem_limit_bytes=60 * 2**20),
+        cost_estimate=pl.CostEstimate(
+            flops=4 * rounds * rows * width * bin_count * lags,
+            bytes_accessed=2 * rounds * rows * width * lags, transcendentals=0),
+    )(own, gathered, table)
+
+
+def shards(spectra, valid_flags):
+    seg_count, blk_count = lax.axis_size("seg"), lax.axis_size("blk")
+    windows_here, width, _, bin_count = spectra.shape
+    rows = width // seg_count
+    fits = 2 * bin_count * rows * width * 4 <= 36 * 2**20
+    if width != 128 or rows % 8 or blk_count % 4 or blk_count < 8 or bin_count % 128 or not fits:
+        return shards_plain(spectra, valid_flags)
+    scaling = 1.0 / math.sqrt(windows_here * seg_count * bin_count)
+    table = jnp.transpose(lag_table(bin_count, LAG_COUNT), (1, 0, 2)).reshape(2 * bin_count, LAG_COUNT)
+    owned = whiten(spectra, valid_flags)
+    padded = -(-windows_here // 16) * 16
+    owned = jnp.pad(owned, ((0, 0), (0, 0), (0, padded - windows_here), (0, 0)))
+    gathered, own_all = exchange(owned, blk_count, seg_count)
+    mine = lax.dynamic_slice_in_dim(own_all, lax.axis_index("seg") * rows, rows, 4)
+    mine = jnp.transpose(mine, (1, 4, 2, 0, 3)).reshape(bin_count, rows, 2 * seg_count * padded)
+    return correlate(mine, gathered, table, scaling)
+
+
 def solution(mesh):
     in_specs = (P("seg", "blk", None, None), P("seg", "blk"))
     out_specs = P(None, ("blk", "seg"), None, None)

time: 399 us -> 353 us (0.88)
  Pallas kernels: 0 us -> 273 us
  waiting for transfers between devices: 165 us -> 0 us
  matrix products: 93 us -> 3.64 us
  other arithmetic: 40.5 us -> 16 us
  local copies, waits for them, and re-layouts: 80.6 us -> 58.5 us
  between operations: 13.5 us -> 0.03 us
  starting transfers between devices: 4.8 us -> 0 us
    pallas_call x0 -> x2, Pallas kernels: none -> 273 us  [the longest x1 141 us: correlate(): pl.pallas_call(functools.partial(correlate_kernel, chunk_count, scaling),...]
    ppermute x2 -> x0, waiting for transfers between devices: 165 us -> none  [passed_along(): return lax.ppermute(value, axis, pairs)]
    dot_general x4 -> x0, matrix products: 89.4 us -> none  [the longest x2 53.7 us: invert(): lax.dot_general(stack, table, (((0, 2), (0, 1)), ((), ())), preferred_ele...]
    reshape x2 -> x1, local copies, waits for them, and re-layouts: 51.4 us -> 13 us  [shards(): jnp.transpose(mine, (1, 4, 2, 0, 3))]
    another operation x2, other arithmetic: 32.2 us -> 10.8 us  [the longest x1 23 us: shards(): return jnp.stack(results)]
    transpose x0 -> x2, local copies, waits for them, and re-layouts: none -> 21.1 us  [shards(): jnp.transpose(mine, (1, 4, 2, 0, 3))]
    ppermute x2 -> x0, local copies, waits for them, and re-layouts: 4.86 us -> none  [passed_along(): return lax.ppermute(value, axis, pairs)]
    ppermute x2 -> x0, starting transfers between devices: 4.76 us -> none  [passed_along(): return lax.ppermute(value, axis, pairs)]
  transfers between devices with their start and end apart: 4 -> 0, of which waited for: 2 -> 0; matrix products, arithmetic and copies ran while one was open for 22% -> 0% of each run, Pallas kernels for 0% -> 0%
where the time goes in v1:
time: 353 us; the launch traced here: 351 us
  Pallas kernels  273 us (77%)
  local copies, waits for them, and re-layouts  58.5 us (17%)
  other arithmetic  16 us (5%)
  matrix products  3.64 us (1%)
    pallas_call x1, Pallas kernels, correlate(): pl.pallas_call(functools.partial(correlate_kernel, chunk_count, scaling),...  141 us
    pallas_call x1, Pallas kernels, exchange(): pl.pallas_call(functools.partial(exchange_kernel, blk_count, seg_count),...  132 us
    transpose x2, local copies, waits for them, and re-layouts, shards(): jnp.transpose(mine, (1, 4, 2, 0, 3))  21.1 us
    reshape x1, local copies, waits for them, and re-layouts, shards(): jnp.transpose(mine, (1, 4, 2, 0, 3))  13 us
    another operation x1, other arithmetic  9.27 us
    slice x1, local copies, waits for them, and re-layouts, whiten(): real_part = spectra[:, :, 0, :].astype(jnp.float32)  8.26 us
    unnamed x1, local copies, waits for them, and re-layouts  8.13 us

profile of v1, /device:TPU:0, one launch (start us, length us, event | category | flops | bytes accessed | tf_op | source)
XLA Modules:
  0.0 350.9 jit_solution(4436053792826393830)
XLA Ops:
  0.0 0.1 convert_reduce_fusion
  0.1 0.7 convert_element_type.48
  0.8 9.3 %cosine_convert_fusion = (bf16[512,1,1024]{2,0,1:T(8,128)(2,1)S(1)}, bf16[512,1,1024]{2,0,1:T(8,128)(2,1)S(1)}) fusion(s32[1024]{0:T(1024)S(1)} %iota_add_fusion, s32[512]{0:T(512)S(1)} %iota_add_fusion.1), kind=kLoop, calls=%fused_computation.10 | loop fusion | flops 6291456 | bytes 2103296 | tf_op jit(solution)/shard_map/convert
  10.1 1.5 pad_maximum_fusion
  11.6 8.1 %copy.6 = bf16[14,128,2,512]{1,0,2,3:T(8,128)(2,1)} copy(bf16[14,128,2,512]{3,2,1,0:T(2,128)(2,1)} %param.2) | data formatting | bytes 7340032 | tf_op args[0]
  19.8 8.3 %fusion.18 = (bf16[14,128,1,512]{3,2,1,0:T(2,128)(2,1)S(1)}, bf16[14,128,1,512]{3,2,1,0:T(2,128)(2,1)S(1)}) fusion(bf16[14,128,2,512]{3,2,1,0:T(2,128)(2,1)} %param.2), kind=kLoop, calls=%fused_computation.26 | loop fusion | bytes 7340032 | tf_op jit(solution)/shard_map/slice | solution.py:35
  28.0 3.6 %add_divide_fusion = f32[14,128,512]{2,1,0:T(8,128)} fusion(f32[512]{0:T(512)S(1)} %convert_reduce_fusion, f32[14,128]{1,0:T(8,128)S(1)} %convert_element_type.48, bf16[14,128,1,512]{3,2,1,0:T(2,128)(2,1)S(1)} %get-tuple-element.10, bf16[14,128,1,512]{3,2,1,0:T(2,128)(2,1)S(1)} %get-tuple-element.9), kind=kOutput, calls=%fused_computation.3 | convolution fusion | flops 948568064 | bytes 7349248 | tf_op jit(solution)/shard_map/dot_general | solution.py:42
  31.7 5.3 %copy.9 = f32[14,128,512]{1,0,2:T(8,128)} copy(f32[14,128,512]{2,1,0:T(8,128)} %add_divide_fusion) | data formatting | bytes 7340032 | tf_op jit(solution)/shard_map/div | solution.py:48
  36.9 4.4 %fusion = bf16[512,2,14,128]{3,2,1,0:T(8,128)(2,1)S(1)} fusion(bf16[14,128,2,512]{1,0,2,3:T(8,128)(2,1)} %copy.6, f32[14,128,512]{1,0,2:T(8,128)} %copy.9), kind=kLoop, calls=%fused_computation.2 | loop fusion | flops 5505024 | bytes 11010048 | tf_op jit(solution)/shard_map/transpose | solution.py:50
  41.3 2.8 pad.4.own
  44.1 132.1 %shard_map.28 = (bf16[2,2,512,2,16,128]{5,4,3,2,1,0:T(8,128)(2,1)}, bf16[2,512,2,16,128]{4,3,2,1,0:T(8,128)(2,1)}, bf16[512,2,16,128]{3,2,1,0:T(8,128)(2,1)}) custom-call(bf16[512,2,16,128]{3,2,1,0:T(8,128)(2,1)} %pad.4.own), custom_call_target="tpu_custom_call" | custom-call | tf_op jit(solution)/shard_map/pallas_call | solution.py:231
  176.3 9.0 %dynamic-slice_bitcast_fusion = bf16[512,64,2,2,16]{1,4,2,0,3:T(8,128)(2,1)} fusion(bf16[2,512,2,16,128]{4,3,2,1,0:T(8,128)(2,1)} %get-tuple-element.7, s32[]{:T(128)S(6)} %select_n.23), kind=kLoop, calls=%fused_computation | loop fusion | bytes 8388612 | tf_op jit(solution)/shard_map/transpose | solution.py:338
  185.3 12.0 %copy.10 = bf16[512,64,2,2,16]{0,4,3,2,1:T(8,128)(2,1)} copy(bf16[512,64,2,2,16]{1,4,2,0,3:T(8,128)(2,1)} %dynamic-slice_bitcast_fusion) | data formatting | bytes 8388608 | tf_op jit(solution)/shard_map/transpose | solution.py:338
  197.3 13.0 %copy.11.own_ref = bf16[512,64,64]{2,1,0:T(8,128)(2,1)} copy(bf16[512,64,64]{0,2,1:T(8,128)(2,1)} %bitcast.18) | data formatting | bytes 8388608 | tf_op jit(solution)/shard_map/reshape | solution.py:338
  210.3 140.6 %shard_map.29 = bf16[2,64,128,1024]{3,2,1,0:T(8,128)(2,1)} custom-call(bf16[512,64,64]{2,1,0:T(8,128)(2,1)} %copy.11.own_ref, bf16[2,2,512,2,16,128]{5,4,3,2,1,0:T(8,128)(2,1)} %get-tuple-element.8.partner_ref, bf16[1024,1024]{1,0:T(8,128)(2,1)} %bitcast.19), custom_call_target="tpu_custom_call" | custom-call | flops 34359738368 | bytes 33554432 | tf_op jit(solution)/shard_map/pallas_call | solution.py:301
  (2 shorter events, 0.0 us)

commit v2 on v1

--- a/solution.py
+++ b/solution.py
@@ -3,6 +3,7 @@
 
 import jax
 import jax.numpy as jnp
+import numpy as np
 from jax import lax
 from jax.experimental import pallas as pl
 from jax.experimental.pallas import tpu as pltpu
@@ -88,7 +89,8 @@
 
 
 PIECES = 8
-ROW_GROUP = 4
+ROW_GROUP = 8
+ROW_PAD = 8
 MESH = pl.DeviceIdType.MESH
 
 
@@ -250,24 +252,42 @@
     return gathered, own_all
 
 
-def correlate_kernel(chunk_count, scaling, own_ref, partner_ref, table_ref, out_ref, cross, left):
+def folded_table(bin_count, lag_count):
+    steps = np.outer(np.arange(bin_count) + BAND_START, np.arange(lag_count) - lag_count // 2) % WIN_SAMPLES
+    angles = steps.astype(np.float32) * np.float32(2.0 * math.pi / WIN_SAMPLES)
+    return jnp.asarray(np.concatenate([np.cos(angles), -np.sin(angles)]), jnp.bfloat16)
+
+
+def correlate_kernel(chunk_count, scaling, own_ref, partner_ref, table_ref, out_ref, cross, left, turned):
     step = pl.program_id(1)
-    bins_here, rows, _ = own_ref.shape
+    segments, bins_here = own_ref.shape[:2]
     width = partner_ref.shape[-1]
-    bin_count = cross.shape[1] // rows
+    bin_count, rows, _ = turned.shape
+    pitch = cross.shape[1] // bin_count
     group = out_ref.shape[1]
+
+    @pl.when((step < chunk_count) & (pl.program_id(0) == 0))
+    def _():
+        mine = pl.ds(pl.multiple_of(lax.axis_index("seg") * rows, 16), rows)
+
+        @pl.loop(0, bins_here, unroll=8)
+        def _(f):
+            stacked = jnp.concatenate(
+                [own_ref[s, f, p] for p in range(2) for s in range(segments)], axis=0)
+            left[pl.ds(0, width), pl.ds(0, stacked.shape[0])] = stacked.T
+            turned[step * bins_here + f] = left[mine, pl.ds(0, stacked.shape[0])]
 
     @pl.when(step < chunk_count)
     def _():
-        @pl.loop(0, bins_here, unroll=8)
+        @pl.loop(0, bins_here, unroll=32)
         def _(f):
-            segments = partner_ref.shape[1]
             real = jnp.concatenate([partner_ref[0, s, f, 0] for s in range(segments)], axis=0)
             imag = jnp.concatenate([partner_ref[0, s, f, 1] for s in range(segments)], axis=0)
             joined = jnp.concatenate(
                 [jnp.concatenate([real, -imag], axis=1), jnp.concatenate([imag, real], axis=1)], axis=0)
-            result = jnp.dot(own_ref[f], joined, preferred_element_type=jnp.float32)
-            start = pl.multiple_of((step * bins_here + f) * rows, 8)
+            result = jnp.dot(
+                turned[step * bins_here + f], joined, preferred_element_type=jnp.float32)
+            start = pl.multiple_of((step * bins_here + f) * pitch, 8)
             cross[0, pl.ds(start, rows), :] = result[:, :width]
             cross[1, pl.ds(start, rows), :] = result[:, width:]
 
@@ -276,7 +296,7 @@
         first = (step - chunk_count) * group
         for n in range(group):
             for k in range(2):
-                picked = cross[k, pl.ds(first + n, bin_count, stride=rows), :]
+                picked = cross[k, pl.ds(first + n, bin_count, stride=pitch), :]
                 left[n * width:(n + 1) * width, k * bin_count:(k + 1) * bin_count] = (
                     picked.astype(jnp.bfloat16).T)
         lags = table_ref.shape[1]
@@ -291,8 +311,8 @@
 
 
 def correlate(own, gathered, table, scaling):
-    bin_count, rows, depth = own.shape
-    rounds, seg_count, _, _, windows, width = gathered.shape
+    rounds, seg_count, bin_count, _, windows, width = gathered.shape
+    rows, depth = width // seg_count, 2 * seg_count * windows
     lags = table.shape[1]
     bins_here = bin_count // 16
     chunk_count = bin_count // bins_here
@@ -303,7 +323,8 @@
         grid=(rounds, steps),
         out_shape=jax.ShapeDtypeStruct((rounds, rows, width, lags), jnp.bfloat16),
         in_specs=[
-            pl.BlockSpec((bins_here, rows, depth), lambda r, t: (jnp.minimum(t, chunk_count - 1), 0, 0)),
+            pl.BlockSpec((seg_count, bins_here, 2, windows, width),
+                         lambda r, t: (0, jnp.where(r == 0, jnp.minimum(t, chunk_count - 1), chunk_count - 1), 0, 0, 0)),
             pl.BlockSpec((1, seg_count, bins_here, 2, windows, width),
                          lambda r, t: (r, 0, jnp.minimum(t, chunk_count - 1), 0, 0, 0)),
             pl.BlockSpec((2 * bin_count, lags), lambda r, t: (0, 0)),
@@ -311,8 +332,9 @@
         out_specs=pl.BlockSpec((1, group, width, lags),
                                lambda r, t: (r, jnp.maximum(t - chunk_count, 0), 0, 0)),
         scratch_shapes=[
-            pltpu.VMEM((2, bin_count * rows, width), jnp.float32),
+            pltpu.VMEM((2, bin_count * (rows + ROW_PAD), width), jnp.float32),
             pltpu.VMEM((group * width, 2 * bin_count), jnp.bfloat16),
+            pltpu.VMEM((bin_count, rows, depth), jnp.bfloat16),
         ],
         compiler_params=pltpu.CompilerParams(vmem_limit_bytes=60 * 2**20),
         cost_estimate=pl.CostEstimate(
@@ -329,14 +351,12 @@
     if width != 128 or rows % 8 or blk_count % 4 or blk_count < 8 or bin_count % 128 or not fits:
         return shards_plain(spectra, valid_flags)
     scaling = 1.0 / math.sqrt(windows_here * seg_count * bin_count)
-    table = jnp.transpose(lag_table(bin_count, LAG_COUNT), (1, 0, 2)).reshape(2 * bin_count, LAG_COUNT)
+    table = folded_table(bin_count, LAG_COUNT)
     owned = whiten(spectra, valid_flags)
     padded = -(-windows_here // 16) * 16
     owned = jnp.pad(owned, ((0, 0), (0, 0), (0, padded - windows_here), (0, 0)))
     gathered, own_all = exchange(owned, blk_count, seg_count)
-    mine = lax.dynamic_slice_in_dim(own_all, lax.axis_index("seg") * rows, rows, 4)
-    mine = jnp.transpose(mine, (1, 4, 2, 0, 3)).reshape(bin_count, rows, 2 * seg_count * padded)
-    return correlate(mine, gathered, table, scaling)
+    return correlate(own_all, gathered, table, scaling)
 
 
 def solution(mesh):

time: 353 us -> 243 us (0.69)
  Pallas kernels: 273 us -> 208 us
  local copies, waits for them, and re-layouts: 58.5 us -> 24.4 us
  other arithmetic: 16 us -> 5.22 us
    pallas_call x1, Pallas kernels: 141 us -> 75.9 us  [correlate(): pl.pallas_call(functools.partial(correlate_kernel, chunk_count, scaling),...]
    transpose x2 -> x0, local copies, waits for them, and re-layouts: 21.1 us -> none  [shards(): jnp.transpose(mine, (1, 4, 2, 0, 3))]
    reshape x1 -> x0, local copies, waits for them, and re-layouts: 13 us -> none  [shards(): jnp.transpose(mine, (1, 4, 2, 0, 3))]
    another operation x2 -> x0, other arithmetic: 10.8 us -> none
where the time goes in v2:
time: 243 us; the launch traced here: 241 us
  Pallas kernels  208 us (86%)
  local copies, waits for them, and re-layouts  24.4 us (10%)
  other arithmetic  5.22 us (2%)
  matrix products  3.63 us (1%)
    pallas_call x1, Pallas kernels, exchange(): pl.pallas_call(functools.partial(exchange_kernel, blk_count, seg_count),...  132 us
    pallas_call x1, Pallas kernels, correlate(): pl.pallas_call(functools.partial(correlate_kernel, chunk_count, scaling),...  75.9 us
    slice x1, local copies, waits for them, and re-layouts, whiten(): real_part = spectra[:, :, 0, :].astype(jnp.float32)  8.26 us
    unnamed x1, local copies, waits for them, and re-layouts  8.13 us
    div x1, local copies, waits for them, and re-layouts, whiten(): scaling = valid_flags.astype(jnp.float32)[:, :, None] / (smooth + 1e-05)  5.26 us

profile of v2, /device:TPU:0, one launch (start us, length us, event | category | flops | bytes accessed | tf_op | source)
XLA Modules:
  0.0 241.4 jit_solution(10599903849980345687)
XLA Ops:
  0.0 0.1 convert_reduce_fusion
  0.1 0.7 convert_element_type.31
  0.8 8.1 %copy.6 = bf16[14,128,2,512]{1,0,2,3:T(8,128)(2,1)} copy(bf16[14,128,2,512]{3,2,1,0:T(2,128)(2,1)} %param.3) | data formatting | bytes 7340032 | tf_op args[0]
  8.9 8.3 %fusion.13 = (bf16[14,128,1,512]{3,2,1,0:T(2,128)(2,1)S(1)}, bf16[14,128,1,512]{3,2,1,0:T(2,128)(2,1)S(1)}) fusion(bf16[14,128,2,512]{3,2,1,0:T(2,128)(2,1)} %param.3), kind=kLoop, calls=%fused_computation.13 | loop fusion | bytes 7340032 | tf_op jit(solution)/shard_map/slice | solution.py:36
  17.2 3.6 %add_divide_fusion = f32[14,128,512]{2,1,0:T(8,128)} fusion(f32[512]{0:T(512)S(1)} %convert_reduce_fusion, f32[14,128]{1,0:T(8,128)S(1)} %convert_element_type.31, bf16[14,128,1,512]{3,2,1,0:T(2,128)(2,1)S(1)} %get-tuple-element.10, bf16[14,128,1,512]{3,2,1,0:T(2,128)(2,1)S(1)} %get-tuple-element.9), kind=kOutput, calls=%fused_computation.2 | convolution fusion | flops 948568064 | bytes 7349248 | tf_op jit(solution)/shard_map/dot_general | solution.py:43
  20.8 5.3 %copy.9 = f32[14,128,512]{1,0,2:T(8,128)} copy(f32[14,128,512]{2,1,0:T(8,128)} %add_divide_fusion) | data formatting | bytes 7340032 | tf_op jit(solution)/shard_map/div | solution.py:49
  26.1 4.4 %fusion = bf16[512,2,14,128]{3,2,1,0:T(8,128)(2,1)S(1)} fusion(bf16[14,128,2,512]{1,0,2,3:T(8,128)(2,1)} %copy.6, f32[14,128,512]{1,0,2:T(8,128)} %copy.9), kind=kLoop, calls=%fused_computation.1 | loop fusion | flops 5505024 | bytes 11010048 | tf_op jit(solution)/shard_map/transpose | solution.py:51
  30.5 2.8 %pad.4.own = bf16[512,2,16,128]{3,2,1,0:T(8,128)(2,1)} pad(bf16[512,2,14,128]{3,2,1,0:T(8,128)(2,1)S(1)} %fusion, bf16[]{:T(256)} %constant.10.clone.1), padding=0_0x0_0x0_2x0_0 | pad | bytes 7864322 | tf_op jit(solution)/shard_map/jit(_pad)/pad | solution.py:357
  33.3 132.1 %shard_map.37 = (bf16[2,2,512,2,16,128]{5,4,3,2,1,0:T(8,128)(2,1)}, bf16[2,512,2,16,128]{4,3,2,1,0:T(8,128)(2,1)}, bf16[512,2,16,128]{3,2,1,0:T(8,128)(2,1)}) custom-call(bf16[512,2,16,128]{3,2,1,0:T(8,128)(2,1)} %pad.4.own), custom_call_target="tpu_custom_call" | custom-call | tf_op jit(solution)/shard_map/pallas_call | solution.py:233
  165.4 75.9 %shard_map.38 = bf16[2,64,128,1024]{3,2,1,0:T(8,128)(2,1)} custom-call(bf16[2,512,2,16,128]{4,3,2,1,0:T(8,128)(2,1)} %get-tuple-element.7.own_ref, bf16[2,2,512,2,16,128]{5,4,3,2,1,0:T(8,128)(2,1)} %get-tuple-element.8.partner_ref, bf16[1024,1024]{1,0:T(8,128)(2,1)} %constant.11.clone.table_ref), custom_call_target="tpu_custom_call" | custom-call | flops 34359738368 | bytes 33554432 | tf_op jit(solution)/shard_map/pallas_call | solution.py:321
